TPU v7x, 32 devices: a whole 2x2x4 slice. The times are simulated.
32 devices in a mesh: req: 4 (over y, x), tile: 8 (over z, core).
Axes of the slice: x: 2, y: 2, z: 4, core: 2. Of those that a mesh axis runs over, the one named last changes fastest.
Arguments:
- image: bfloat16 [8, 4096, 2432], P('req', 'tile'), may hold values from -40 to 40
- text: bfloat16 [8, 154, 2432], P('req'), may hold values from -40 to 40
- pooled: float32 [8, 2432], P('req'), may hold values from -6 to 6
- timesteps: int32 [8], P('req'), may hold values from 0 to 999
- lengths: int32 [8], P('req'), may hold values from 1 to 4096, 16384 in all
- w_time: bfloat16 [256, 2432], replicated, may hold values from -0.375 to 0.375
- w_mod: bfloat16 [2432, 9728], P(None, 'tile'), may hold values from -0.125 to 0.125
- w_img: bfloat16 [2432, 6144], P(None, ('req', 'tile')), may hold values from -0.125 to 0.125
- w_txt: bfloat16 [2432, 6144], P(None, 'tile'), may hold values from -0.125 to 0.125
- q_gain: float32 [64], replicated, may hold values from 1 to 2.5
- k_gain: float32 [64], replicated, may hold values from 1 to 2.5
- text_q_gain: float32 [64], replicated, may hold values from 1 to 2.5
- text_k_gain: float32 [64], replicated, may hold values from 1 to 2.5
Outputs:
- image_attention: bfloat16 [8, 4096, 2048], P('req', 'tile')
- text_attention: bfloat16 [8, 154, 2048], P('req', None, 'tile')
Inputs may be any that keep to these rules, and one draw needn't show every extreme that they name: `lengths`: the image token counts of all 8 requests sum to 16384, and the largest is exactly 4096.
All inputs are finite; a program needn't handle non-finite values. No bound on the sum of `lengths` on one device may be relied on, other than what follows from the above.
Results may differ from a plain program's by a relative error of at most 0.02.
Values may be sent and summed in bfloat16 or wider, within the bound.
No kernel may reach another device: no remote copies, remote signals or barrier semaphores. Data moves between devices by JAX's collectives and lax.ppermute only.
A program may use at most 192 MiB of HBM per device.

v0:
```python
import math

import jax
import jax.numpy as jnp
from jax import lax
from jax.sharding import PartitionSpec as P

epsilon = 1e-06


def time_features(step_index, feature_count):
    half_count = feature_count // 2
    frequency = jnp.exp(-math.log(10000.0) * jnp.arange(half_count, dtype=jnp.float32) / half_count)
    angles = step_index.astype(jnp.float32)[:, None] * frequency[None, :]
    return jnp.concatenate([jnp.cos(angles), jnp.sin(angles)], axis=-1).astype(jnp.bfloat16)


def modulate(tokens, shift, scale):
    values = tokens.astype(jnp.float32)
    center = jnp.mean(values, axis=-1, keepdims=True)
    spread = jnp.mean(jnp.square(values - center), axis=-1, keepdims=True)
    normed = (values - center) * lax.rsqrt(spread + epsilon)
    return (normed * (1.0 + scale.astype(jnp.float32)) + shift.astype(jnp.float32)).astype(
        jnp.bfloat16
    )


def rms_gain(vectors, gain):
    factor = lax.rsqrt(jnp.mean(jnp.square(vectors), axis=-1, keepdims=True) + epsilon)
    return (vectors * factor * gain).astype(jnp.bfloat16)


def pack_heads(qkv, head_dim, q_gain, k_gain):
    lead = qkv.shape[:2]
    head_count = qkv.shape[-1] // (3 * head_dim)
    qkv = qkv.reshape(lead + (head_count, 3, head_dim))
    return jnp.concatenate(
        [
            rms_gain(qkv[:, :, :, 0:1, :], q_gain),
            rms_gain(qkv[:, :, :, 1:2, :], k_gain),
            qkv[:, :, :, 2:3, :].astype(jnp.bfloat16),
        ],
        axis=3,
    ).reshape(lead + (head_count, 3 * head_dim))


def local(
    image,
    text,
    pooled,
    timesteps,
    lengths,
    w_time,
    w_mod,
    w_img,
    w_txt,
    q_gain,
    k_gain,
    text_q_gain,
    text_k_gain,
):
    tile_count = lax.axis_size("tile")
    group_count, local_rows, model_width = image.shape
    seq_len = local_rows * tile_count
    text_len = text.shape[1]
    head_dim = q_gain.shape[0]
    heads_here = w_txt.shape[1] // (3 * head_dim)
    score_scale = head_dim ** (-0.5)
    block = min(512, seq_len)
    features = time_features(timesteps, w_time.shape[0])
    cond_act = jax.nn.silu(
        pooled + jnp.dot(features, w_time, preferred_element_type=jnp.float32)
    ).astype(jnp.bfloat16)
    mod_part = jnp.dot(cond_act, w_mod, preferred_element_type=jnp.float32).astype(jnp.bfloat16)
    modulation = lax.all_gather(mod_part, "tile", axis=1, tiled=True)
    h_img = modulate(
        image,
        modulation[:, None, 0:model_width],
        modulation[:, None, model_width : 2 * model_width],
    )
    qkv_img = jnp.einsum(
        "gpd,dc->gpc",
        h_img,
        lax.all_gather(w_img, ("req", "tile"), axis=1, tiled=True),
        preferred_element_type=jnp.float32,
    )
    packed = pack_heads(qkv_img, head_dim, q_gain, k_gain)
    by_head = lax.all_to_all(packed, "tile", split_axis=2, concat_axis=1, tiled=True)
    by_head = by_head.reshape(group_count, seq_len, heads_here, 3, head_dim)
    h_txt = modulate(
        text,
        modulation[:, None, 2 * model_width : 3 * model_width],
        modulation[:, None, 3 * model_width : 4 * model_width],
    )
    qkv_txt = jnp.einsum("gtd,dc->gtc", h_txt, w_txt, preferred_element_type=jnp.float32).reshape(
        group_count, text_len, heads_here, 3, head_dim
    )
    text_queries = jnp.moveaxis(rms_gain(qkv_txt[:, :, :, 0, :], text_q_gain), 2, 1)
    text_keys = jnp.moveaxis(rms_gain(qkv_txt[:, :, :, 1, :], text_k_gain), 2, 1)
    text_values = jnp.moveaxis(qkv_txt[:, :, :, 2, :].astype(jnp.bfloat16), 2, 1)
    image_queries = jnp.moveaxis(by_head[:, :, :, 0, :], 2, 1)
    image_keys = jnp.moveaxis(by_head[:, :, :, 1, :], 2, 1)
    image_values = jnp.moveaxis(by_head[:, :, :, 2, :], 2, 1)
    slot_live = (jnp.arange(seq_len, dtype=jnp.int32)[None, :] < lengths[:, None]).astype(
        jnp.float32
    )
    keys = jnp.concatenate([text_keys, image_keys], axis=2)
    values = jnp.concatenate([text_values, image_values], axis=2)
    key_mask = jnp.concatenate([jnp.ones((group_count, text_len), jnp.float32), slot_live], axis=1)

    def attend_block(query_block):
        scores = (
            jnp.einsum("ghqe,ghke->ghqk", query_block, keys, preferred_element_type=jnp.float32)
            * score_scale
        )
        weights = jnp.exp(scores) * key_mask[:, None, None, :]
        total = jnp.sum(weights, axis=-1)
        summed = jnp.einsum(
            "ghqk,ghke->ghqe",
            weights.astype(jnp.bfloat16),
            values,
            preferred_element_type=jnp.float32,
        )
        return summed / total[..., None]

    text_result = attend_block(text_queries)
    block_count = seq_len // block
    query_blocks = jnp.moveaxis(
        image_queries.reshape(group_count, heads_here, block_count, block, head_dim), 2, 0
    )
    image_result = lax.map(attend_block, query_blocks)
    image_result = jnp.moveaxis(image_result, 0, 2).reshape(
        group_count, heads_here, seq_len, head_dim
    )
    image_result = image_result * slot_live[:, None, :, None]
    image_heads = (
        jnp.moveaxis(image_result, 1, 2)
        .reshape(group_count, seq_len, heads_here * head_dim)
        .astype(jnp.bfloat16)
    )
    image_attention = lax.all_to_all(image_heads, "tile", split_axis=1, concat_axis=2, tiled=True)
    text_attention = (
        jnp.moveaxis(text_result, 1, 2)
        .reshape(group_count, text_len, heads_here * head_dim)
        .astype(jnp.bfloat16)
    )
    return (image_attention, text_attention)


def solution(mesh):
    in_specs = (
        P("req", "tile", None),
        P("req", None, None),
        P("req", None),
        P("req"),
        P("req"),
        P(),
        P(None, "tile"),
        P(None, ("req", "tile")),
        P(None, "tile"),
        P(),
        P(),
        P(),
        P(),
    )
    out_specs = (P("req", "tile", None), P("req", None, "tile"))
    return jax.shard_map(local, mesh=mesh, in_specs=in_specs, out_specs=out_specs, check_vma=False)
```

profile of v0, /device:TPU:0, one launch (start us, length us, event | category | flops | bytes accessed | tf_op | source)
XLA Modules:
  0.0 1161.0 jit_solution(908466781604082626)
XLA Ops:
  13.2 15.8 %all-gather = bf16[8,1216,2]{1,2,0:T(2,128)(2,1)S(1)} all-gather(bf16[1,1216,2]{1,2,0:T(2,128)(2,1)S(1)} %fusion.45), channel_id=1, replica_groups=mesh['req'=4,'tile'=8] {'tile'}, dimensions={0}, use_global_device_ids=true | all-gather | bytes 43776 | tf_op jit(solution)/shard_map/all_gather | solution.py:75
  36.2 155.0 %all-gather.3.cloned.1.call-done = bf16[2432,6144]{0,1:T(8,128)(2,1)} async-done(((bf16[2432,192]{0,1:T(8,128)(2,1)}), bf16[2432,6144]{0,1:T(8,128)(2,1)}) %all-gather.3.cloned.1.call-update) | async-done | bytes 29884432 | tf_op jit(solution)/shard_map/all_gather | solution.py:84
  191.2 40.7 %fusion.18 = f32[2,512,6144]{1,2,0:T(8,128)} fusion(bf16[2432,6144]{0,1:T(8,128)(2,1)} %all-gather.3.cloned.1.call-done, bf16[2,512,2432]{2,1,0:T(8,128)(2,1)} %param.15, f32[2,2432]{1,0:T(2,128)S(1)} %get-tuple-element.67, f32[2,2432]{1,0:T(2,128)S(1)} %get-tuple-element.65, f32[2,512]{1,0:T(2,128)S(1)} %add_rsqrt_fusion.5, ...), kind=kOutput, calls=%fused_computation.12 | convolution fusion | flops 30616584192 | bytes 60078080 | tf_op jit(solution)/shard_map/gpd,dc->gpc/dot_general | solution.py:81
  274.0 263.1 %all-to-all-done = bf16[2,512,32,192]{1,3,0,2:T(8,128)(2,1)} async-done(((bf16[2,512,32,192]{1,3,0,2:T(8,128)(2,1)}), bf16[2,512,32,192]{1,3,0,2:T(8,128)(2,1)}, u32[]{:S(2)}, u32[]{:S(2)}) %all-to-all-start) | async-done | bytes 12582944 | tf_op jit(solution)/shard_map/all_to_all | solution.py:88
  537.1 14.5 %copy.54 = bf16[2,8,512,4,192]{2,1,4,3,0:T(8,128)(2,1)} copy(bf16[2,8,512,4,192]{2,4,0,3,1:T(8,128)(2,1)} %bitcast.10) | data formatting | bytes 25165824 | tf_op jit(solution)/shard_map/all_to_all | solution.py:88
  551.5 19.5 %reshape.144 = bf16[2,4096,4,3,64]{1,4,3,2,0:T(8,128)(2,1)} reshape(bf16[2,8,512,4,192]{2,1,4,3,0:T(8,128)(2,1)} %copy.54) | data formatting | bytes 25165824 | tf_op jit(solution)/shard_map/reshape | solution.py:89
  588.4 430.8 %while.10 = (s32[]{:T(128)}, f32[8,2,4,512,64]{3,4,2,1,0:T(8,128)}, bf16[8,2,4,512,64]{3,4,2,1,0:T(8,128)(2,1)}, bf16[2,4,4250,64]{2,3,1,0:T(8,128)(2,1)}, f32[2...) while((s32[]{:T(128)}, f32[8,2,4,512,64]{3,4,2,1,0:T(8,128)}, ...), condition=%wide.region_9.10_spmd, body=%wide.region_7.0_spmd.sunk | while | flops 4561154048 | bytes 149949936 | solution.py:131
  588.4 27.6 %fusion.92 = (f32[2,4,512]{2,1,0:T(4,128)S(1)}, f32[2,4,512,4250]{2,3,1,0:T(8,128)}) fusion(f32[2,4250]{1,0:T(2,128)S(1)} %get-tuple-element.133, bf16[2,4,4250,64]{2,3,1,0:T(8,128)(2,1)} %get-tuple-element.132, bf16[8,2,4,512,64]{3,4,2,1,0:T(8,128)(2,1)} %get-tuple-element.131, s32[]{:T(128)} %get-tuple-element.122), kind=kOutput, calls=%fused_computation.1.clone.1 | convolution fusion | flops 2280443904 | bytes 74663632 | tf_op jit(solution)/shard_map/while/body/eval_jaxpr/ghqe,ghke->ghqk/dot_general | solution.py:113
  616.0 26.2 %fusion.93 = f32[8,2,4,512,64]{3,4,2,1,0:T(8,128)} fusion(f32[8,2,4,512,64]{3,4,2,1,0:T(8,128)} %get-tuple-element.123, s32[]{:T(128)} %get-tuple-element.122, bf16[2,4,4250,64]{2,3,1,0:T(8,128)(2,1)} %get-tuple-element.134, f32[2,4,512,4250]{2,3,1,0:T(8,128)} %get-tuple-element.113, f32[2,4250]{1,0:T(2,128)S(1)} %get-tuple-element.133, ...), kind=kOutput, calls=%fused_computation.6.clone.1 | convolution fusion | flops 2280710144 | bytes 75286224 | tf_op jit(solution)/shard_map/while/body/eval_jaxpr/ghqk,ghke->ghqe/dot_general | solution.py:118
  642.2 27.6 %fusion.92 = (f32[2,4,512]{2,1,0:T(4,128)S(1)}, f32[2,4,512,4250]{2,3,1,0:T(8,128)}) fusion(f32[2,4250]{1,0:T(2,128)S(1)} %get-tuple-element.133, bf16[2,4,4250,64]{2,3,1,0:T(8,128)(2,1)} %get-tuple-element.132, bf16[8,2,4,512,64]{3,4,2,1,0:T(8,128)(2,1)} %get-tuple-element.131, s32[]{:T(128)} %get-tuple-element.122), kind=kOutput, calls=%fused_computation.1.clone.1 | convolution fusion | flops 2280443904 | bytes 74663632 | tf_op jit(solution)/shard_map/while/body/eval_jaxpr/ghqe,ghke->ghqk/dot_general | solution.py:113
  669.8 26.2 %fusion.93 = f32[8,2,4,512,64]{3,4,2,1,0:T(8,128)} fusion(f32[8,2,4,512,64]{3,4,2,1,0:T(8,128)} %get-tuple-element.123, s32[]{:T(128)} %get-tuple-element.122, bf16[2,4,4250,64]{2,3,1,0:T(8,128)(2,1)} %get-tuple-element.134, f32[2,4,512,4250]{2,3,1,0:T(8,128)} %get-tuple-element.113, f32[2,4250]{1,0:T(2,128)S(1)} %get-tuple-element.133, ...), kind=kOutput, calls=%fused_computation.6.clone.1 | convolution fusion | flops 2280710144 | bytes 75286224 | tf_op jit(solution)/shard_map/while/body/eval_jaxpr/ghqk,ghke->ghqe/dot_general | solution.py:118
  696.0 27.6 %fusion.92 = (f32[2,4,512]{2,1,0:T(4,128)S(1)}, f32[2,4,512,4250]{2,3,1,0:T(8,128)}) fusion(f32[2,4250]{1,0:T(2,128)S(1)} %get-tuple-element.133, bf16[2,4,4250,64]{2,3,1,0:T(8,128)(2,1)} %get-tuple-element.132, bf16[8,2,4,512,64]{3,4,2,1,0:T(8,128)(2,1)} %get-tuple-element.131, s32[]{:T(128)} %get-tuple-element.122), kind=kOutput, calls=%fused_computation.1.clone.1 | convolution fusion | flops 2280443904 | bytes 74663632 | tf_op jit(solution)/shard_map/while/body/eval_jaxpr/ghqe,ghke->ghqk/dot_general | solution.py:113
  723.6 26.2 %fusion.93 = f32[8,2,4,512,64]{3,4,2,1,0:T(8,128)} fusion(f32[8,2,4,512,64]{3,4,2,1,0:T(8,128)} %get-tuple-element.123, s32[]{:T(128)} %get-tuple-element.122, bf16[2,4,4250,64]{2,3,1,0:T(8,128)(2,1)} %get-tuple-element.134, f32[2,4,512,4250]{2,3,1,0:T(8,128)} %get-tuple-element.113, f32[2,4250]{1,0:T(2,128)S(1)} %get-tuple-element.133, ...), kind=kOutput, calls=%fused_computation.6.clone.1 | convolution fusion | flops 2280710144 | bytes 75286224 | tf_op jit(solution)/shard_map/while/body/eval_jaxpr/ghqk,ghke->ghqe/dot_general | solution.py:118
  749.8 27.6 %fusion.92 = (f32[2,4,512]{2,1,0:T(4,128)S(1)}, f32[2,4,512,4250]{2,3,1,0:T(8,128)}) fusion(f32[2,4250]{1,0:T(2,128)S(1)} %get-tuple-element.133, bf16[2,4,4250,64]{2,3,1,0:T(8,128)(2,1)} %get-tuple-element.132, bf16[8,2,4,512,64]{3,4,2,1,0:T(8,128)(2,1)} %get-tuple-element.131, s32[]{:T(128)} %get-tuple-element.122), kind=kOutput, calls=%fused_computation.1.clone.1 | convolution fusion | flops 2280443904 | bytes 74663632 | tf_op jit(solution)/shard_map/while/body/eval_jaxpr/ghqe,ghke->ghqk/dot_general | solution.py:113
  777.5 26.2 %fusion.93 = f32[8,2,4,512,64]{3,4,2,1,0:T(8,128)} fusion(f32[8,2,4,512,64]{3,4,2,1,0:T(8,128)} %get-tuple-element.123, s32[]{:T(128)} %get-tuple-element.122, bf16[2,4,4250,64]{2,3,1,0:T(8,128)(2,1)} %get-tuple-element.134, f32[2,4,512,4250]{2,3,1,0:T(8,128)} %get-tuple-element.113, f32[2,4250]{1,0:T(2,128)S(1)} %get-tuple-element.133, ...), kind=kOutput, calls=%fused_computation.6.clone.1 | convolution fusion | flops 2280710144 | bytes 75286224 | tf_op jit(solution)/shard_map/while/body/eval_jaxpr/ghqk,ghke->ghqe/dot_general | solution.py:118
  803.7 27.6 %fusion.92 = (f32[2,4,512]{2,1,0:T(4,128)S(1)}, f32[2,4,512,4250]{2,3,1,0:T(8,128)}) fusion(f32[2,4250]{1,0:T(2,128)S(1)} %get-tuple-element.133, bf16[2,4,4250,64]{2,3,1,0:T(8,128)(2,1)} %get-tuple-element.132, bf16[8,2,4,512,64]{3,4,2,1,0:T(8,128)(2,1)} %get-tuple-element.131, s32[]{:T(128)} %get-tuple-element.122), kind=kOutput, calls=%fused_computation.1.clone.1 | convolution fusion | flops 2280443904 | bytes 74663632 | tf_op jit(solution)/shard_map/while/body/eval_jaxpr/ghqe,ghke->ghqk/dot_general | solution.py:113
  831.3 26.2 %fusion.93 = f32[8,2,4,512,64]{3,4,2,1,0:T(8,128)} fusion(f32[8,2,4,512,64]{3,4,2,1,0:T(8,128)} %get-tuple-element.123, s32[]{:T(128)} %get-tuple-element.122, bf16[2,4,4250,64]{2,3,1,0:T(8,128)(2,1)} %get-tuple-element.134, f32[2,4,512,4250]{2,3,1,0:T(8,128)} %get-tuple-element.113, f32[2,4250]{1,0:T(2,128)S(1)} %get-tuple-element.133, ...), kind=kOutput, calls=%fused_computation.6.clone.1 | convolution fusion | flops 2280710144 | bytes 75286224 | tf_op jit(solution)/shard_map/while/body/eval_jaxpr/ghqk,ghke->ghqe/dot_general | solution.py:118
  857.5 27.6 %fusion.92 = (f32[2,4,512]{2,1,0:T(4,128)S(1)}, f32[2,4,512,4250]{2,3,1,0:T(8,128)}) fusion(f32[2,4250]{1,0:T(2,128)S(1)} %get-tuple-element.133, bf16[2,4,4250,64]{2,3,1,0:T(8,128)(2,1)} %get-tuple-element.132, bf16[8,2,4,512,64]{3,4,2,1,0:T(8,128)(2,1)} %get-tuple-element.131, s32[]{:T(128)} %get-tuple-element.122), kind=kOutput, calls=%fused_computation.1.clone.1 | convolution fusion | flops 2280443904 | bytes 74663632 | tf_op jit(solution)/shard_map/while/body/eval_jaxpr/ghqe,ghke->ghqk/dot_general | solution.py:113
  885.1 26.2 %fusion.93 = f32[8,2,4,512,64]{3,4,2,1,0:T(8,128)} fusion(f32[8,2,4,512,64]{3,4,2,1,0:T(8,128)} %get-tuple-element.123, s32[]{:T(128)} %get-tuple-element.122, bf16[2,4,4250,64]{2,3,1,0:T(8,128)(2,1)} %get-tuple-element.134, f32[2,4,512,4250]{2,3,1,0:T(8,128)} %get-tuple-element.113, f32[2,4250]{1,0:T(2,128)S(1)} %get-tuple-element.133, ...), kind=kOutput, calls=%fused_computation.6.clone.1 | convolution fusion | flops 2280710144 | bytes 75286224 | tf_op jit(solution)/shard_map/while/body/eval_jaxpr/ghqk,ghke->ghqe/dot_general | solution.py:118
  911.3 27.6 %fusion.92 = (f32[2,4,512]{2,1,0:T(4,128)S(1)}, f32[2,4,512,4250]{2,3,1,0:T(8,128)}) fusion(f32[2,4250]{1,0:T(2,128)S(1)} %get-tuple-element.133, bf16[2,4,4250,64]{2,3,1,0:T(8,128)(2,1)} %get-tuple-element.132, bf16[8,2,4,512,64]{3,4,2,1,0:T(8,128)(2,1)} %get-tuple-element.131, s32[]{:T(128)} %get-tuple-element.122), kind=kOutput, calls=%fused_computation.1.clone.1 | convolution fusion | flops 2280443904 | bytes 74663632 | tf_op jit(solution)/shard_map/while/body/eval_jaxpr/ghqe,ghke->ghqk/dot_general | solution.py:113
  938.9 26.2 %fusion.93 = f32[8,2,4,512,64]{3,4,2,1,0:T(8,128)} fusion(f32[8,2,4,512,64]{3,4,2,1,0:T(8,128)} %get-tuple-element.123, s32[]{:T(128)} %get-tuple-element.122, bf16[2,4,4250,64]{2,3,1,0:T(8,128)(2,1)} %get-tuple-element.134, f32[2,4,512,4250]{2,3,1,0:T(8,128)} %get-tuple-element.113, f32[2,4250]{1,0:T(2,128)S(1)} %get-tuple-element.133, ...), kind=kOutput, calls=%fused_computation.6.clone.1 | convolution fusion | flops 2280710144 | bytes 75286224 | tf_op jit(solution)/shard_map/while/body/eval_jaxpr/ghqk,ghke->ghqe/dot_general | solution.py:118
  965.1 27.6 %fusion.92 = (f32[2,4,512]{2,1,0:T(4,128)S(1)}, f32[2,4,512,4250]{2,3,1,0:T(8,128)}) fusion(f32[2,4250]{1,0:T(2,128)S(1)} %get-tuple-element.133, bf16[2,4,4250,64]{2,3,1,0:T(8,128)(2,1)} %get-tuple-element.132, bf16[8,2,4,512,64]{3,4,2,1,0:T(8,128)(2,1)} %get-tuple-element.131, s32[]{:T(128)} %get-tuple-element.122), kind=kOutput, calls=%fused_computation.1.clone.1 | convolution fusion | flops 2280443904 | bytes 74663632 | tf_op jit(solution)/shard_map/while/body/eval_jaxpr/ghqe,ghke->ghqk/dot_general | solution.py:113
  992.8 26.2 %fusion.93 = f32[8,2,4,512,64]{3,4,2,1,0:T(8,128)} fusion(f32[8,2,4,512,64]{3,4,2,1,0:T(8,128)} %get-tuple-element.123, s32[]{:T(128)} %get-tuple-element.122, bf16[2,4,4250,64]{2,3,1,0:T(8,128)(2,1)} %get-tuple-element.134, f32[2,4,512,4250]{2,3,1,0:T(8,128)} %get-tuple-element.113, f32[2,4250]{1,0:T(2,128)S(1)} %get-tuple-element.133, ...), kind=kOutput, calls=%fused_computation.6.clone.1 | convolution fusion | flops 2280710144 | bytes 75286224 | tf_op jit(solution)/shard_map/while/body/eval_jaxpr/ghqk,ghke->ghqe/dot_general | solution.py:118
  1065.6 70.9 %all-to-all-done.1 = bf16[2,4096,256]{2,0,1:T(2,128)(2,1)} async-done(((bf16[2,4096,256]{2,0,1:T(2,128)(2,1)}), bf16[2,4096,256]{2,0,1:T(2,128)(2,1)}, u32[]{:S(2)}, u32[]{:S(2)}) %all-to-all-start.1) | async-done | bytes 4194336 | tf_op jit(solution)/shard_map/all_to_all | solution.py:141
  (90 shorter events, 135.9 us)
Async XLA Ops:
  7.2 1.5 copy-start
  7.2 184.0 %all-gather.3.cloned.1.call-start = ((), (), s32[]{:S(2)}) async-start(), calls=%async_computation.2 | async-start | bytes 30818304 | tf_op jit(solution)/shard_map/all_gather | solution.py:84
  239.1 4.1 copy-start.14
  239.1 4.1 copy-start.15
  257.6 5.7 copy-start.16
  257.6 6.4 copy-start.5
  257.6 279.4 %all-to-all-start = ((bf16[2,512,32,192]{1,3,0,2:T(8,128)(2,1)}), bf16[2,512,32,192]{1,3,0,2:T(8,128)(2,1)}, u32[]{:S(2)}, u32[]{:S(2)}) async-start(bf16[2,512,32,192]{1,3,0,2:T(8,128)(2,1)} %copy.52), calls=%async_computation | async-start | bytes 25165824 | tf_op jit(solution)/shard_map/all_to_all | solution.py:88
  263.3 7.1 copy-start.18
  263.4 0.6 copy-start.12
  270.4 3.5 copy-start.17
  272.6 1.2 copy-start.6
  273.9 310.3 %copy-start.8 = (bf16[2,4,154,64]{2,3,1,0:T(8,128)(2,1)}, bf16[2,4,154,64]{2,3,1,0:T(8,128)(2,1)S(1)}, u32[]{:S(2)}) copy-start(bf16[2,4,154,64]{2,3,1,0:T(8,128)(2,1)S(1)} %fusion.60) | copy-start | bytes 473092
  274.0 305.8 %copy-start.10 = (bf16[2,4,154,64]{2,3,1,0:T(8,128)(2,1)}, bf16[2,4,154,64]{2,3,1,0:T(8,128)(2,1)S(1)}, u32[]{:S(2)}) copy-start(bf16[2,4,154,64]{2,3,1,0:T(8,128)(2,1)S(1)} %fusion.56) | copy-start | bytes 473092
  576.7 7.4 copy-start.4
  576.8 7.4 copy-start.2
  1019.2 4.4 copy-start.13
  1037.8 4.7 copy-start.7
  1037.8 4.8 copy-start.11
  1037.8 4.8 copy-start.19
  1037.8 98.7 %all-to-all-start.1 = ((bf16[2,4096,256]{2,0,1:T(2,128)(2,1)}), bf16[2,4096,256]{2,0,1:T(2,128)(2,1)}, u32[]{:S(2)}, u32[]{:S(2)}) async-start(bf16[2,4096,256]{2,0,1:T(2,128)(2,1)} %copy.63), calls=%async_computation.1 | async-start | bytes 8388608 | tf_op jit(solution)/shard_map/all_to_all | solution.py:141
  1042.6 11.9 %copy-start.3 = (bf16[2,4,4096,64]{2,3,1,0:T(8,128)(2,1)S(1)}, bf16[2,4,4096,64]{2,3,1,0:T(8,128)(2,1)}, u32[]{:S(2)}) copy-start(bf16[2,4,4096,64]{2,3,1,0:T(8,128)(2,1)} %copy-done.2) | copy-start | bytes 12582916
  1042.6 11.9 %copy-start.9 = (bf16[2,4,154,64]{2,3,1,0:T(8,128)(2,1)S(1)}, bf16[2,4,154,64]{2,3,1,0:T(8,128)(2,1)}, u32[]{:S(2)}) copy-start(bf16[2,4,154,64]{2,3,1,0:T(8,128)(2,1)} %copy-done.8) | copy-start | bytes 473092
  1141.2 12.5 %copy-start.1 = (bf16[256,2432]{1,0:T(8,128)(2,1)S(1)}, bf16[256,2432]{1,0:T(8,128)(2,1)}, u32[]{:S(2)}) copy-start(bf16[256,2432]{1,0:T(8,128)(2,1)} %param.20) | copy-start | bytes 3735556
Sparse Core Ops, SparseCore 0:
  11.0 180.0 all-gather.2
where the time goes:
time: 1170 us; the launch traced here: 1160 us
  matrix products  500 us (43%)
  waiting for transfers between devices  490 us (42%)
  local copies, waits for them, and re-layouts  87.3 us (7%)
  other arithmetic  42.7 us (4%)
  blocking collectives  15.8 us (1%)
  between operations  14.9 us (1%)
    all_to_all x1, waiting for transfers between devices, local(): lax.all_to_all(packed, 'tile', split_axis=2, concat_axis=1, tiled=True)  263 us
    dot_general x9, matrix products, attend_block(): jnp.einsum('ghqe,ghke->ghqk', query_block, keys, preferred_element_type=j...  233 us
    dot_general x9, matrix products, attend_block(): jnp.einsum('ghqk,ghke->ghqe', weights.astype(jnp.bfloat16), values, prefe...  220 us
    all_gather x1, waiting for transfers between devices, local(): lax.all_gather(w_img, ('req', 'tile'), axis=1, tiled=True)  155 us
    all_to_all x1, waiting for transfers between devices, local(): lax.all_to_all(image_heads, 'tile', split_axis=1, concat_axis=2, tiled=True)  70.9 us
    dot_general x1, matrix products, local(): jnp.einsum('gpd,dc->gpc', h_img, lax.all_gather(w_img, ('req', 'tile'), a...  40.7 us
  transfers between devices with their start and end apart: 3, of which 3 were waited for; matrix products, arithmetic and copies ran while one was open for 4% of the time, Pallas kernels for 0%

commit v1 on v0

v1 whole, which is shorter than its diff:
```python
import functools, math
import jax, jax.numpy as jnp
from jax import lax
from jax.experimental import pallas as pl
from jax.experimental.pallas import tpu as pltpu
from jax.sharding import PartitionSpec as P

def attend_kernel(block, tail, masked, len_ref, q_ref, k_ref, v_ref, tk_ref, tv_ref, *refs):
    rows = pl.program_id(1)
    length = len_ref[0]
    out_ref = refs[-1]
    many = out_ref.shape[0]
    chunks = length // block
    rest = (length - chunks * block + tail - 1) // tail
    half = q_ref.shape[1] // 2

    def weigh(queries, keys, values):
        scores = jnp.dot(keys, queries, preferred_element_type=jnp.float32)
        return jnp.dot(
            values, jnp.exp2(scores).astype(jnp.bfloat16), preferred_element_type=jnp.float32
        )

    def run(queries):
        def body(size, first, c, carry):
            here = pl.ds(pl.multiple_of(first + c * size, size), size)
            return tuple(
                carry[h] + weigh(queries, k_ref[h, here, :], v_ref[h, :, here]) for h in range(2)
            )

        carry = tuple(weigh(queries, tk_ref[h], tv_ref[h]) for h in range(2))
        carry = lax.fori_loop(0, chunks, functools.partial(body, block, 0), carry)
        carry = lax.fori_loop(0, rest, functools.partial(body, tail, chunks * block), carry)
        out = jnp.concatenate([sums[0:half] / sums[half : half + 1] for sums in carry], axis=0)
        return jnp.transpose(out)

    if not masked:
        out_ref[...] = run(q_ref[0]).astype(jnp.bfloat16)
        return

    @pl.when(rows * many < length)
    def _():
        result = run(q_ref[0])
        spot = rows * many + lax.broadcasted_iota(jnp.int32, result.shape, 0)
        out_ref[...] = jnp.where(spot < length, result, 0.0).astype(jnp.bfloat16)

    @pl.when(rows * many >= length)
    def _():
        out_ref[...] = jnp.zeros_like(out_ref)


def attend(length, q, k, v, tk, tv, first, last, seq, many, block, tail, masked, shared, earlier=None):
    pairs, width, rows = q.shape
    rows = min(rows, seq)
    text_keys = tk.shape[1]
    into = first if shared else 0
    operands = [length, q, k, v, tk, tv]
    aliases = {}
    if earlier is not None:
        aliases = {len(operands): 0}
        operands.append(earlier)
    columns = (pairs if shared else last - first) * width

    def live(r, s):
        return jnp.minimum(r, (s[0] + many - 1) // many - 1) if masked else r

    return pl.pallas_call(
        functools.partial(attend_kernel, block, tail, masked),
        grid_spec=pltpu.PrefetchScalarGridSpec(
            num_scalar_prefetch=1,
            grid=(last - first, rows // many),
            in_specs=[
                pl.BlockSpec((1, width, many), lambda p, r, s: (p + first, 0, live(r, s))),
                pl.BlockSpec((2, seq, width), lambda p, r, s: (p + first, 0, 0)),
                pl.BlockSpec((2, width, seq), lambda p, r, s: (p + first, 0, 0)),
                pl.BlockSpec((2, text_keys, width), lambda p, r, s: (p + first, 0, 0)),
                pl.BlockSpec((2, width, text_keys), lambda p, r, s: (p + first, 0, 0)),
            ]
            + [pl.BlockSpec(memory_space=pl.ANY) for _ in aliases],
            out_specs=pl.BlockSpec((many, width), lambda p, r, s: (r, p + into)),
        ),
        out_shape=jax.ShapeDtypeStruct((rows, columns), jnp.bfloat16),
        input_output_aliases=aliases,
        compiler_params=pltpu.CompilerParams(
            dimension_semantics=("arbitrary", "arbitrary"), vmem_limit_bytes=48 << 20
        ),
        cost_estimate=pl.CostEstimate(
            flops=(last - first) * 16 * rows * seq * width,
            bytes_accessed=(last - first) * 8 * seq * width,
            transcendentals=(last - first) * 2 * rows * seq,
        ),
        name="attend",
    )(*operands)


def arrange_kernel(head_dim, parts, order_ref, *refs):
    out_ref = refs[-1]
    width = 2 * head_dim
    tiles = refs[0].shape[0]
    start = 0
    for ref in refs[:parts]:
        for p in range(ref.shape[2] // width):
            for e in range(2):
                here = slice(p * width + e * head_dim, p * width + (e + 1) * head_dim)
                for a in range(tiles // 2):
                    both = [ref[2 * a, :, here], ref[2 * a + 1, :, here]]
                    out_ref[0, :, start : start + width] = jnp.concatenate(both, axis=1)
                    start += width


def arrange(place, parts, earlier, group_count, rows, head_dim):
    tiles, local_rows, _ = parts[0].shape
    operands = [place, *parts]
    aliases = {}
    if earlier is not None:
        aliases = {len(operands): 0}
        operands.append(earlier)
    total = sum(tiles * part.shape[2] for part in parts)
    return pl.pallas_call(
        functools.partial(arrange_kernel, head_dim, len(parts)),
        grid_spec=pltpu.PrefetchScalarGridSpec(
            num_scalar_prefetch=1,
            grid=(local_rows // rows,),
            in_specs=[
                pl.BlockSpec((tiles, rows, part.shape[2]), lambda r, s: (0, r, 0)) for part in parts
            ]
            + [pl.BlockSpec(memory_space=pl.ANY) for _ in aliases],
            out_specs=pl.BlockSpec((1, rows, total), lambda r, s: (s[0], r, 0)),
        ),
        out_shape=jax.ShapeDtypeStruct((group_count, local_rows, total), jnp.bfloat16),
        input_output_aliases=aliases,
        compiler_params=pltpu.CompilerParams(
            dimension_semantics=("arbitrary",), vmem_limit_bytes=48 << 20
        ),
        cost_estimate=pl.CostEstimate(
            flops=0, bytes_accessed=4 * local_rows * total, transcendentals=0
        ),
        name="arrange",
    )(*operands)


def project_kernel(head_dim, cover, arrays, chunks, spot_ref, *refs):
    x_refs = refs[:arrays]
    mod_ref, wq_ref, wk_ref, wv_ref, gain_ref, sum_ref = refs[arrays : arrays + 6]
    q_ref, k_ref, v_ref, held = refs[-4:]
    step = pl.program_id(0)
    rows = held.shape[0]
    length = spot_ref[chunks]
    spot = spot_ref[step]
    start = spot * rows

    @pl.when((spot >= 0) & (start < (length + cover - 1) // cover * cover))
    def _():
        if arrays == 1:
            x = x_refs[0][...].astype(jnp.float32)
        else:
            for i in range(arrays):

                @pl.when(step == i)
                def _():
                    held[...] = x_refs[i][...]

            x = held[...].astype(jnp.float32)
        depth = x.shape[1]
        center = jnp.sum(x, axis=1, keepdims=True) * (1.0 / depth)
        x = x - center
        spread = jnp.sum(x * x, axis=1, keepdims=True) * (1.0 / depth)
        h = x * lax.rsqrt(spread + epsilon)
        h = (h * (1.0 + mod_ref[1:2, :]) + mod_ref[0:1, :]).astype(jnp.bfloat16)

        def norm(values, gain):
            squares = values * values
            high = squares.astype(jnp.bfloat16)
            low = (squares - high.astype(jnp.float32)).astype(jnp.bfloat16)
            total = jnp.dot(high, sum_ref[...], preferred_element_type=jnp.float32)
            total = total + jnp.dot(low, sum_ref[...], preferred_element_type=jnp.float32)
            return (values * lax.rsqrt(total * (1.0 / head_dim) + epsilon) * gain).astype(
                jnp.bfloat16
            )

        width = 2 * head_dim
        q = norm(jnp.dot(h, wq_ref[...], preferred_element_type=jnp.float32), gain_ref[0:1, :])
        k = norm(jnp.dot(h, wk_ref[...], preferred_element_type=jnp.float32), gain_ref[1:2, :])
        v = jnp.dot(h, wv_ref[...], preferred_element_type=jnp.float32).astype(jnp.bfloat16)
        qt, vt = jnp.transpose(q), jnp.transpose(v)
        lane = lax.broadcasted_iota(jnp.int32, (rows, width), 1)
        live = start + lax.broadcasted_iota(jnp.int32, (head_dim, rows), 1) < length
        none = jnp.zeros((head_dim, rows), jnp.bfloat16)
        one = jnp.where(live, jnp.ones_like(none), none)
        gap = jnp.zeros((rows, width), jnp.bfloat16)
        for p in range(q.shape[1] // width):
            here = slice(p * width, (p + 1) * width)
            q_ref[p] = qt[here]
            k_ref[2 * p] = jnp.where(lane < head_dim, k[:, here], gap)
            k_ref[2 * p + 1] = jnp.where(lane < head_dim, gap, k[:, here])
            for h in (2 * p, 2 * p + 1):
                v_ref[h, 0:head_dim] = jnp.where(live, vt[h * head_dim : (h + 1) * head_dim], none)
                v_ref[h, head_dim:width] = one


def project(length, spots, tokens, mod, weights, gains, sums, seq, cover, head_dim, earlier):
    arrays, chunks = len(tokens), len(spots)
    depth = tokens[0].shape[1]
    rows = tokens[0].shape[0] * arrays // chunks
    cols = weights[0].shape[1]
    heads = cols // head_dim
    width = 2 * head_dim
    blocks = seq // rows
    scalars = jnp.concatenate([jnp.stack(spots).astype(jnp.int32), length])

    def place(i, s):
        spot = s[i]
        used = (spot >= 0) & (spot * rows < (s[chunks] + cover - 1) // cover * cover)
        return jnp.where(used, spot, blocks)

    def row(i, s):
        last = (s[chunks] + cover - 1) // cover * (cover // rows) - 1
        return (jnp.minimum(i, last) if arrays == 1 else 0, 0)

    def whole(a):
        return pl.BlockSpec(a.shape, lambda i, s: (0,) * a.ndim)

    constants = [mod, *weights, gains, sums]
    operands = [scalars, *tokens, *constants]
    aliases = {}
    if earlier is not None:
        aliases = {len(operands) + i: i for i in range(3)}
        operands += list(earlier)
    padded = seq + max(rows, 128)
    return pl.pallas_call(
        functools.partial(project_kernel, head_dim, cover, arrays, chunks),
        grid_spec=pltpu.PrefetchScalarGridSpec(
            num_scalar_prefetch=1,
            grid=(chunks,),
            in_specs=[pl.BlockSpec((rows, depth), row) for _ in tokens]
            + [whole(a) for a in constants]
            + [pl.BlockSpec(memory_space=pl.ANY) for _ in aliases],
            out_specs=[
                pl.BlockSpec((heads // 2, width, rows), lambda i, s: (0, 0, place(i, s))),
                pl.BlockSpec((heads, rows, width), lambda i, s: (0, place(i, s), 0)),
                pl.BlockSpec((heads, width, rows), lambda i, s: (0, 0, place(i, s))),
            ],
            scratch_shapes=[pltpu.VMEM((rows, depth), jnp.bfloat16)],
        ),
        out_shape=[
            jax.ShapeDtypeStruct((heads // 2, width, padded), jnp.bfloat16),
            jax.ShapeDtypeStruct((heads, padded, width), jnp.bfloat16),
            jax.ShapeDtypeStruct((heads, width, padded), jnp.bfloat16),
        ],
        input_output_aliases=aliases,
        compiler_params=pltpu.CompilerParams(
            dimension_semantics=("arbitrary",), vmem_limit_bytes=48 << 20
        ),
        cost_estimate=pl.CostEstimate(
            flops=6 * chunks * rows * depth * cols,
            bytes_accessed=2 * (chunks * rows * depth + 3 * depth * cols),
            transcendentals=chunks * rows,
        ),
        name="project",
    )(*operands)


epsilon = 1e-06


def time_features(step_index, feature_count):
    half_count = feature_count // 2
    frequency = jnp.exp(-math.log(10000.0) * jnp.arange(half_count, dtype=jnp.float32) / half_count)
    angles = step_index.astype(jnp.float32)[:, None] * frequency[None, :]
    return jnp.concatenate([jnp.cos(angles), jnp.sin(angles)], axis=-1).astype(jnp.bfloat16)


def modulate(tokens, shift, scale):
    values = tokens.astype(jnp.float32)
    center = jnp.mean(values, axis=-1, keepdims=True)
    spread = jnp.mean(jnp.square(values - center), axis=-1, keepdims=True)
    normed = (values - center) * lax.rsqrt(spread + epsilon)
    return (normed * (1.0 + scale.astype(jnp.float32)) + shift.astype(jnp.float32)).astype(
        jnp.bfloat16
    )


def rms_gain(vectors, gain):
    factor = lax.rsqrt(jnp.mean(jnp.square(vectors), axis=-1, keepdims=True) + epsilon)
    return (vectors * factor * gain).astype(jnp.bfloat16)


def gather_req(shard):
    count = lax.axis_size("req")
    if count & (count - 1):
        return lax.all_gather(shard, "req", axis=0)
    mine = lax.axis_index("req")
    shards = [shard]
    for step in range(1, count):
        shards.append(lax.ppermute(shard, "req", [(i, i ^ step) for i in range(count)]))
    stacked = jnp.stack(shards)
    return jnp.stack(
        [lax.dynamic_index_in_dim(stacked, mine ^ i, 0, keepdims=False) for i in range(count)]
    )


def head_weights(w_img, head_dim, heads_here):
    width = 3 * head_dim
    if strided(w_img, head_dim, heads_here):
        shards = gather_req(w_img)
        depth = shards.shape[1]
        shards = shards.reshape(heads_here, depth, 3, head_dim)
    else:
        whole = lax.all_gather(w_img, ("req", "tile"), axis=1, tiled=True)
        depth = whole.shape[0]
        start = lax.axis_index("tile") * heads_here * width
        part = lax.dynamic_slice_in_dim(whole, start, heads_here * width, axis=1)
        shards = jnp.moveaxis(part.reshape(depth, heads_here, 3, head_dim), 1, 0)
    shards = jnp.pad(shards, ((0, heads_here % 2), (0, 0), (0, 0), (0, 0)))
    return jnp.transpose(shards, (2, 1, 0, 3)).reshape(3, depth, -1)


def strided(w_img, head_dim, heads_here):
    return (
        w_img.shape[1] == 3 * head_dim
        and heads_here == lax.axis_size("req")
        and lax.axis_size("tile") % heads_here == 0
    )


def text_to_strided(qkv):
    tiles, mine, heads = lax.axis_size("tile"), lax.axis_index("tile"), qkv.shape[2]
    folds = tiles // heads
    parts = jnp.moveaxis(qkv, 2, 0)
    pick = (jnp.arange(folds) == mine % folds)[:, None, None, None, None]
    send = jnp.where(pick, parts[None], jnp.zeros_like(parts[None]))
    send = send.reshape((tiles,) + parts.shape[1:])
    got = lax.all_to_all(send, "tile", split_axis=0, concat_axis=0, tiled=True)
    got = got.reshape((heads, folds) + parts.shape[1:])
    return jnp.moveaxis(
        lax.dynamic_index_in_dim(got, mine // heads, 1, keepdims=False), 0, 2
    )


def text_from_strided(out, head_dim):
    tiles, mine = lax.axis_size("tile"), lax.axis_index("tile")
    groups, text_len, width = out.shape
    heads = width // head_dim
    folds = tiles // heads
    parts = jnp.moveaxis(out.reshape(groups, text_len, heads, head_dim), 2, 0)
    pick = (jnp.arange(folds) == mine // heads)[None, :, None, None, None]
    send = jnp.where(pick, parts[:, None], jnp.zeros_like(parts[:, None]))
    send = send.reshape((tiles,) + parts.shape[1:])
    got = lax.all_to_all(send, "tile", split_axis=0, concat_axis=0, tiled=True)
    got = got.reshape((folds, heads) + parts.shape[1:])
    got = lax.dynamic_index_in_dim(got, mine % folds, 0, keepdims=False)
    return jnp.moveaxis(got, 0, 2).reshape(groups, text_len, width)


def after(values, *others):
    return lax.optimization_barrier((values, others))[0]


class Spread:
    def __init__(self, tokens):
        self.tiles, self.mine = lax.axis_size("tile"), lax.axis_index("tile")
        self.pair = 2 if self.tiles % 2 == 0 else 1
        self.steps = self.tiles // self.pair
        self.right = self.left = tokens
        self.done = 0
        self.found = [self.both(tokens, self.mine)]

    def both(self, chunk, source):
        valid = (source >= 0) & (source < self.tiles)
        found = [(chunk, jnp.where(valid, source, -1))]
        if self.pair == 2:
            source = source + 1 - 2 * (self.mine % 2)
            swap = [(i, i ^ 1) for i in range(self.tiles)]
            found.append((lax.ppermute(chunk, "tile", swap), jnp.where(valid, source, -1)))
        return found

    def step(self, *others):
        if others:
            self.right, self.left = after((self.right, self.left), *others)
        pairs = [(i, i + self.pair) for i in range(self.tiles - self.pair)]
        self.right = lax.ppermute(self.right, "tile", pairs)
        self.left = lax.ppermute(self.left, "tile", [(j, i) for i, j in pairs])
        self.done += 1
        offset = self.pair * self.done
        self.found.append(
            self.both(self.right, self.mine - offset) + self.both(self.left, self.mine + offset)
        )


def text_operands(qkv, head_dim, rows, keys):
    text_len, heads = qkv.shape[0], qkv.shape[1]
    turned = jnp.transpose(qkv, (1, 2, 0))
    queries = turned[:, 0:head_dim].reshape(heads // 2, 2 * head_dim, text_len)
    queries = jnp.pad(queries, ((0, 0), (0, 0), (0, rows - text_len)))
    even = (jnp.arange(heads) % 2 == 0)[:, None, None]
    key = jnp.moveaxis(qkv[:, :, head_dim : 2 * head_dim], 1, 0)
    none = jnp.zeros_like(key)
    key = jnp.concatenate([jnp.where(even, key, none), jnp.where(even, none, key)], axis=2)
    key = jnp.pad(key, ((0, 0), (0, keys - text_len), (0, 0)))
    value = turned[:, 2 * head_dim : 3 * head_dim]
    value = jnp.concatenate([value, jnp.ones_like(value)], axis=1)
    value = jnp.pad(value, ((0, 0), (0, 0), (0, keys - text_len)))
    return queries, key, value


def local(
    image,
    text,
    pooled,
    timesteps,
    lengths,
    w_time,
    w_mod,
    w_img,
    w_txt,
    q_gain,
    k_gain,
    text_q_gain,
    text_k_gain,
):
    tiles = lax.axis_size("tile")
    group_count, local_rows, model_width = image.shape
    seq_len = local_rows * tiles
    text_len = text.shape[1]
    head_dim = q_gain.shape[0]
    heads_here = w_txt.shape[1] // (3 * head_dim)
    spare = heads_here % 2
    width = (heads_here + spare) * head_dim
    query_factor = head_dim ** (-0.5) * math.log2(math.e)
    text_rows = -(-text_len // 128) * 128
    text_keys = -(-text_len // 128) * 128
    by_stride = strided(w_img, head_dim, heads_here)

    if group_count == 2:
        longer = (lengths[1] > lengths[0]).astype(jnp.int32)
        order = undo = jnp.stack([longer, 1 - longer])
    else:
        order = jnp.argsort(-lengths)
        undo = jnp.argsort(order)
    sorted_lengths = lengths[order]
    tokens = [
        lax.dynamic_index_in_dim(image, order[slot], 0, keepdims=False)
        for slot in range(group_count)
    ]
    first = Spread(tokens[0])
    first.step()

    features = time_features(timesteps, w_time.shape[0])
    cond_act = jax.nn.silu(
        pooled + jnp.dot(features, w_time, preferred_element_type=jnp.float32)
    ).astype(jnp.bfloat16)
    mod_part = jnp.dot(cond_act, w_mod, preferred_element_type=jnp.float32).astype(jnp.bfloat16)
    modulation = lax.all_to_all(
        jnp.broadcast_to(mod_part[None], (tiles,) + mod_part.shape),
        "tile",
        split_axis=0,
        concat_axis=0,
        tiled=True,
    )
    modulation = jnp.moveaxis(modulation, 0, 1)
    modulation = modulation.reshape(group_count, 4, model_width)

    weights = head_weights(w_img, head_dim, heads_here)
    gains = jnp.stack(
        [
            jnp.tile(q_gain * query_factor, heads_here + spare),
            jnp.tile(k_gain, heads_here + spare),
        ]
    )
    group_of = jnp.arange(width) // head_dim
    sums = (group_of[:, None] == group_of[None, :]).astype(jnp.bfloat16)

    h_txt = modulate(text, modulation[:, None, 2], modulation[:, None, 3])
    qkv_txt = jnp.einsum("gtd,dc->gtc", h_txt, w_txt, preferred_element_type=jnp.float32).reshape(
        group_count, text_len, heads_here, 3, head_dim
    )
    text_qkv = jnp.concatenate(
        [
            rms_gain(qkv_txt[:, :, :, 0, :], text_q_gain * query_factor),
            rms_gain(qkv_txt[:, :, :, 1, :], text_k_gain),
            qkv_txt[:, :, :, 2, :].astype(jnp.bfloat16),
        ],
        axis=-1,
    )
    local_text = text_qkv
    if by_stride:
        text_qkv = text_to_strided(text_qkv)
    text_qkv = jnp.pad(text_qkv, ((0, 0), (0, 0), (0, spare), (0, 0)))

    cover = min(512, seq_len)
    block = min(1024, seq_len)
    pairs = width // (2 * head_dim)
    lengths_of, mods, text_parts = [], [], []
    for slot in range(group_count):
        lengths_of.append(lax.dynamic_slice_in_dim(sorted_lengths, slot, 1))
        mod = lax.dynamic_index_in_dim(modulation, order[slot], 0, keepdims=False)
        mods.append(mod[0:2].astype(jnp.float32))
        one = lax.dynamic_index_in_dim(text_qkv, order[slot], 0, keepdims=False)
        text_parts.append(text_operands(one, head_dim, text_rows, text_keys))

    def project_step(slot, found, earlier):
        return project(
            lengths_of[slot],
            [source for _, source in found],
            [chunk for chunk, _ in found],
            mods[slot],
            [weights[i] for i in range(3)],
            gains,
            sums,
            seq_len,
            cover,
            head_dim,
            earlier,
        )

    def attend_text(slot, packed):
        query, key, value = text_parts[slot]
        operands = (lengths_of[slot], query, packed[1], packed[2], key, value)
        out = attend(*operands, 0, pairs, seq_len, text_rows, block, cover, False, True)
        return out[0:text_len, 0 : heads_here * head_dim]

    def attend_image(slot, packed, start, stop, many, shared, earlier=None):
        _, key, value = text_parts[slot]
        operands = (lengths_of[slot], *packed, key, value)
        return attend(
            *operands, start, stop, seq_len, many, block, cover, True, shared, earlier
        )

    def send_back(out):
        out = out[:, 0 : heads_here * head_dim].reshape(tiles, local_rows, -1)
        return lax.all_to_all(out, "tile", split_axis=0, concat_axis=0, tiled=True)

    image_attention = None
    image_back, text_outs = [], []
    spreading = first
    waiting = [mod_part]
    packed = None
    for slot in range(group_count):
        latest = slot == group_count - 1
        if slot > 0:
            following = Spread(after(tokens[slot], spreading.right, spreading.left))
            following.step(packed)
            waiting = []
            previous, before = packed, spreading
            for found in before.found[consumed:]:
                previous = project_step(slot - 1, found, previous)
            waiting.append([previous])
            out = None
            for pair in range(pairs):
                out = attend_image(slot - 1, previous, pair, pair + 1, block, True, out)
                waiting.append([out])
            text_outs.append(attend_text(slot - 1, previous))
            image_back.append([send_back(out)])
            spreading = following
            packed = None
            consumed = 0
            for step in range(2, spreading.steps):
                spreading.step(*(waiting[step - 2] if step - 2 < len(waiting) else []))
            packed = project_step(slot, after(spreading.found[0], *waiting[-1]), None)
            consumed = 1
        else:
            spreading.step(mod_part)
            for step in range(3, spreading.steps):
                spreading.step(*([weights, local_text] if step == 3 else []))
            packed = project_step(slot, spreading.found[0], None)
            packed = project_step(slot, spreading.found[1], packed)
            consumed = 2
        if latest:
            for found in spreading.found[consumed:]:
                packed = project_step(slot, found, packed)
            text_outs.append(attend_text(slot, packed))
            text_attention = jnp.stack(text_outs)[undo]
            if by_stride:
                text_attention = text_from_strided(text_attention, head_dim)
            parts = []
            for pair in range(pairs):
                out = attend_image(slot, packed, pair, pair + 1, cover, False)
                parts.append(send_back(out))
            image_back.append(parts)

    if by_stride:
        for slot, parts in enumerate(image_back):
            place = lax.dynamic_slice_in_dim(order, slot, 1)
            image_attention = arrange(
                place, parts, image_attention, group_count, min(128, local_rows), head_dim
            )
    else:
        image_attention = jnp.stack(
            [
                jnp.concatenate(
                    [part.reshape(tiles, local_rows, -1, head_dim) for part in parts], axis=2
                )
                for parts in image_back
            ]
        )[undo]
        image_attention = jnp.transpose(image_attention, (0, 2, 1, 3, 4)).reshape(
            group_count, local_rows, tiles * heads_here * head_dim
        )
    return (image_attention, text_attention)


def solution(mesh):
    in_specs = (
        P("req", "tile", None),
        P("req", None, None),
        P("req", None),
        P("req"),
        P("req"),
        P(),
        P(None, "tile"),
        P(None, ("req", "tile")),
        P(None, "tile"),
        P(),
        P(),
        P(),
        P(),
    )
    out_specs = (P("req", "tile", None), P("req", None, "tile"))
    return jax.shard_map(local, mesh=mesh, in_specs=in_specs, out_specs=out_specs, check_vma=False)
```

time: 1170 us -> 631 us (0.54)
  matrix products: 500 us -> 8.88 us
  waiting for transfers between devices: 490 us -> 198 us
  Pallas kernels: 0 us -> 260 us
  starting transfers between devices: 10.4 us -> 82.6 us
  local copies, waits for them, and re-layouts: 87.3 us -> 58.8 us
  other arithmetic: 42.7 us -> 18 us
  blocking collectives: 15.8 us -> 0 us
    dot_general x19 -> x0, matrix products: 493 us -> none  [the longest x9 233 us: attend_block(): jnp.einsum('ghqe,ghke->ghqk', query_block, keys, preferred_element_type=j...]
    all_to_all x2 -> x6, waiting for transfers between devices: 334 us -> 58.3 us  [the longest x1 34.1 us: local(): lax.all_to_all(jnp.broadcast_to(mod_part[None], (tiles,) + mod_part.shape...]
    pallas_call x0 -> x16, Pallas kernels: none -> 260 us  [the longest x6 140 us: attend(): pl.pallas_call(functools.partial(attend_kernel, block, tail, masked), gri...]
    all_gather x1 -> x0, waiting for transfers between devices: 155 us -> none  [local(): lax.all_gather(w_img, ('req', 'tile'), axis=1, tiled=True)]
    ppermute x0 -> x29, waiting for transfers between devices: none -> 140 us  [the longest x6 85 us: step(): self.right = lax.ppermute(self.right, 'tile', pairs)]
    ppermute x0 -> x29, starting transfers between devices: none -> 52.7 us  [the longest x6 35.8 us: step(): self.right = lax.ppermute(self.right, 'tile', pairs)]
    reshape x4 -> x2, local copies, waits for them, and re-layouts: 32 us -> 0.29 us  [the longest x1 0.19 us: text_from_strided(): parts = jnp.moveaxis(out.reshape(groups, text_len, heads, head_dim), 2, 0)]
    all_to_all x3 -> x1, local copies, waits for them, and re-layouts: 25.5 us -> 1.5 us  [text_to_strided(): got = lax.all_to_all(send, 'tile', split_axis=0, concat_axis=0, tiled=True)]
  transfers between devices with their start and end apart: 3 -> 35, of which waited for: 3 -> 14; matrix products, arithmetic and copies ran while one was open for 4% -> 9% of each run, Pallas kernels for 0% -> 41%
where the time goes in v1:
time: 631 us; the launch traced here: 630 us
  Pallas kernels  260 us (41%)
  waiting for transfers between devices  198 us (31%)
  starting transfers between devices  82.6 us (13%)
  local copies, waits for them, and re-layouts  58.8 us (9%)
  other arithmetic  18 us (3%)
  matrix products  8.88 us (1%)
    pallas_call x6, Pallas kernels, attend(): pl.pallas_call(functools.partial(attend_kernel, block, tail, masked), gri...  140 us
    pallas_call x8, Pallas kernels, project(): pl.pallas_call(functools.partial(project_kernel, head_dim, cover, arrays,...  114 us
    ppermute x6, waiting for transfers between devices, step(): self.right = lax.ppermute(self.right, 'tile', pairs)  85 us
    ppermute x6, starting transfers between devices, step(): self.right = lax.ppermute(self.right, 'tile', pairs)  35.8 us
    all_to_all x1, waiting for transfers between devices, local(): lax.all_to_all(jnp.broadcast_to(mod_part[None], (tiles,) + mod_part.shape...  34.1 us
    ppermute x6, waiting for transfers between devices, step(): self.left = lax.ppermute(self.left, 'tile', [(j, i) for i, j in pairs])  29.3 us
    unnamed x91, local copies, waits for them, and re-layouts  26.3 us
    ppermute x3, waiting for transfers between devices, gather_req(): lax.ppermute(shard, 'req', [(i, i ^ step) for i in range(count)])  25.8 us
  transfers between devices with their start and end apart: 35, of which 14 were waited for; matrix products, arithmetic and copies ran while one was open for 9% of the time, Pallas kernels for 41%

profile of v1, /device:TPU:0, one launch (start us, length us, event | category | flops | bytes accessed | tf_op | source)
XLA Modules:
  0.0 630.1 jit_solution(2050533144686023045)
XLA Ops:
  21.6 6.0 all-to-all-start
  40.2 34.1 %all-to-all-done = bf16[8,2,1216]{2,1,0:T(2,128)(2,1)S(1)} async-done(((bf16[8,2,1216]{2,1,0:T(2,128)(2,1)}), bf16[8,2,1216]{2,1,0:T(2,128)(2,1)S(1)}, u32[]{:S(2)}, u32[]{:S(2)}) %all-to-all-start) | async-done | bytes 38944 | tf_op jit(solution)/shard_map/all_to_all | solution.py:452
  87.4 43.2 %collective-permute-done.2.refs_0_ = bf16[512,2432]{1,0:T(8,128)(2,1)} collective-permute-done((bf16[512,2432]{1,0:T(8,128)(2,1)}, bf16[512,2432]{1,0:T(8,128)(2,1)}, u32[]{:S(2)}, u32[]{:S(2)}) %collective-permute-start.2) | collective-permute-done | bytes 2490400 | tf_op jit(solution)/shard_map/ppermute | solution.py:380
  146.6 25.8 %collective-permute-done.9 = bf16[2432,192]{0,1:T(8,128)(2,1)} collective-permute-done((bf16[2432,192]{0,1:T(8,128)(2,1)}, bf16[2432,192]{0,1:T(8,128)(2,1)}, u32[]{:S(2)}, u32[]{:S(2)}) %collective-permute-start.9) | collective-permute-done | bytes 933920 | tf_op jit(solution)/shard_map/ppermute | solution.py:294
  195.8 15.0 %project.8 = (bf16[2,128,4608]{2,1,0:T(8,128)(2,1)}, bf16[4,4608,128]{2,1,0:T(8,128)(2,1)}, bf16[4,128,4608]{2,1,0:T(8,128)(2,1)}) custom-call(s32[3]{0:T(128)S(1)} %pad_add_fusion.spot_ref, bf16[512,2432]{1,0:T(8,128)(2,1)} %get-tuple-element.88.refs_0_, bf16[512,2432]{1,0:T(8,128)(2,1)} %collective-permute-done.11.refs_1_, ...), custom_call_target="tpu_custom_call" | custom-call | flops 3825205248 | bytes 8716288 | tf_op jit(solution)/shard_map/project/pallas_call | solution.py:229
  210.9 17.7 %collective-permute-done.4.refs_0_ = bf16[512,2432]{1,0:T(8,128)(2,1)} collective-permute-done((bf16[512,2432]{1,0:T(8,128)(2,1)}, bf16[512,2432]{1,0:T(8,128)(2,1)}, u32[]{:S(2)}, u32[]{:S(2)}) %collective-permute-start.4) | collective-permute-done | bytes 2490400 | tf_op jit(solution)/shard_map/ppermute | solution.py:380
  234.1 16.5 %project.9 = (bf16[2,128,4608]{2,1,0:T(8,128)(2,1)}, bf16[4,4608,128]{2,1,0:T(8,128)(2,1)}, bf16[4,128,4608]{2,1,0:T(8,128)(2,1)}) custom-call(s32[5]{0:T(128)S(1)} %concatenate.65.spot_ref, bf16[512,2432]{1,0:T(8,128)(2,1)} %collective-permute-done.refs_0_, ...), custom_call_target="tpu_custom_call", output_to_operand_aliasing={{0}: (11, {}), {1}: (12, {}), {2}: (13, {})} | custom-call | flops 7650410496 | bytes 13697024 | tf_op jit(solution)/shard_map/project/pallas_call | solution.py:229
  250.6 14.2 %collective-permute-start.12 = (bf16[512,2432]{1,0:T(8,128)(2,1)}, bf16[512,2432]{1,0:T(8,128)(2,1)}, u32[]{:S(2)}, u32[]{:S(2)}) collective-permute-start(bf16[512,2432]{1,0:T(8,128)(2,1)} %get-tuple-element.66.refs_0_), channel_id=1, source_target_pairs={{0,2},{1,3},{2,4},{3,5},{4,6},{5,7},{8,10},{9,11},{10,12},{11,13},... | collective-permute-start | bytes 7471112 | tf_op jit(solution)/shard_map/ppermute | solution.py:380
  279.4 16.5 %project.10 = (bf16[2,128,4608]{2,1,0:T(8,128)(2,1)}, bf16[4,4608,128]{2,1,0:T(8,128)(2,1)}, bf16[4,128,4608]{2,1,0:T(8,128)(2,1)}) custom-call(s32[5]{0:T(128)S(1)} %concatenate.68.spot_ref, bf16[512,2432]{1,0:T(8,128)(2,1)} %collective-permute-done.2.refs_0_, ...), custom_call_target="tpu_custom_call", output_to_operand_aliasing={{0}: (11, {}), {1}: (12, {}), {2}: (13, {})} | custom-call | flops 7650410496 | bytes 13697024 | tf_op jit(solution)/shard_map/project/pallas_call | solution.py:229
  296.0 16.5 %project.11 = (bf16[2,128,4608]{2,1,0:T(8,128)(2,1)}, bf16[4,4608,128]{2,1,0:T(8,128)(2,1)}, bf16[4,128,4608]{2,1,0:T(8,128)(2,1)}) custom-call(s32[5]{0:T(128)S(1)} %concatenate.67.spot_ref, bf16[512,2432]{1,0:T(8,128)(2,1)} %collective-permute-done.4.refs_0_, ...), custom_call_target="tpu_custom_call", output_to_operand_aliasing={{0}: (11, {}), {1}: (12, {}), {2}: (13, {})} | custom-call | flops 7650410496 | bytes 13697024 | tf_op jit(solution)/shard_map/project/pallas_call | solution.py:229
  329.4 37.4 %attend.6.refs_0_ = bf16[4096,256]{1,0:T(8,128)(2,1)S(1)} custom-call(s32[1]{0:T(128)} %get-tuple-element.115.len_ref, bf16[2,128,4608]{2,1,0:T(8,128)(2,1)S(1)} %copy-done.23, bf16[4,4608,128]{2,1,0:T(8,128)(2,1)} %get-tuple-element.58.k_ref, bf16[4,128,4608]{2,1,0:T(8,128)(2,1)} %get-tuple-element.59.v_ref, bf16[4,256,128]{2,1,0:T(8,128)(2,1)S(1)} %copy-done.17, ...), custom_call_target="tpu_custom_call" | custom-call | flops 34359738368 | bytes 4194304 | tf_op jit(solution)/shard_map/attend/pallas_call | solution.py:66
  367.4 10.6 %collective-permute-done.18.refs_0_ = bf16[512,2432]{1,0:T(8,128)(2,1)} collective-permute-done((bf16[512,2432]{1,0:T(8,128)(2,1)}, bf16[512,2432]{1,0:T(8,128)(2,1)}, u32[]{:S(2)}, u32[]{:S(2)}) %collective-permute-start.18) | collective-permute-done | bytes 2490400 | tf_op jit(solution)/shard_map/ppermute | solution.py:380
  388.4 37.7 %attend.7 = bf16[4096,256]{1,0:T(8,128)(2,1)S(1)} custom-call(s32[1]{0:T(128)} %get-tuple-element.115.len_ref, bf16[2,128,4608]{2,1,0:T(8,128)(2,1)S(1)} %copy-done.23, bf16[4,4608,128]{2,1,0:T(8,128)(2,1)} %get-tuple-element.58.k_ref, bf16[4,128,4608]{2,1,0:T(8,128)(2,1)} %get-tuple-element.59.v_ref, ...), custom_call_target="tpu_custom_call", output_to_operand_aliasing={{}: (6, {})} | custom-call | flops 34359738368 | bytes 4194304 | tf_op jit(solution)/shard_map/attend/pallas_call | solution.py:66
  431.7 8.2 %collective-permute-done.20.refs_0_ = bf16[512,2432]{1,0:T(8,128)(2,1)} collective-permute-done((bf16[512,2432]{1,0:T(8,128)(2,1)}, bf16[512,2432]{1,0:T(8,128)(2,1)}, u32[]{:S(2)}, u32[]{:S(2)}) %collective-permute-start.20) | collective-permute-done | bytes 2490400 | tf_op jit(solution)/shard_map/ppermute | solution.py:380
  439.9 8.6 %collective-permute-done.22.refs_2_ = bf16[512,2432]{1,0:T(8,128)(2,1)} collective-permute-done((bf16[512,2432]{1,0:T(8,128)(2,1)}, bf16[512,2432]{1,0:T(8,128)(2,1)}, u32[]{:S(2)}, u32[]{:S(2)}) %collective-permute-start.22) | collective-permute-done | bytes 2490400 | tf_op jit(solution)/shard_map/ppermute | solution.py:381
  453.6 11.9 %attend.10 = bf16[256,256]{1,0:T(8,128)(2,1)S(1)} custom-call(s32[1]{0:T(128)} %get-tuple-element.115.len_ref, bf16[2,128,256]{2,1,0:T(8,128)(2,1)S(1)} %copy-done.20, bf16[4,4608,128]{2,1,0:T(8,128)(2,1)S(1)} %copy-done.21, bf16[4,128,4608]{2,1,0:T(8,128)(2,1)} %get-tuple-element.59.v_ref, bf16[4,256,128]{2,1,0:T(8,128)(2,1)S(1)} %copy-done.18, ...), custom_call_target="tpu_custom_call" | custom-call | flops 4294967296 | bytes 8388608 | tf_op jit(solution)/shard_map/attend/pallas_call | solution.py:66
  466.2 15.1 %project.12 = (bf16[2,128,4608]{2,1,0:T(8,128)(2,1)}, bf16[4,4608,128]{2,1,0:T(8,128)(2,1)}, bf16[4,128,4608]{2,1,0:T(8,128)(2,1)}) custom-call(s32[3]{0:T(128)S(1)} %pad_add_fusion.1.spot_ref, bf16[512,2432]{1,0:T(8,128)(2,1)} %get-tuple-element.66.refs_0_, bf16[512,2432]{1,0:T(8,128)(2,1)} %copy-done.36, f32[2,2432]{1,0:T(2,128)S(1)} %get-tuple-element.109.refs_2_.refs_4_, ...), custom_call_target="tpu_custom_call" | custom-call | flops 3825205248 | bytes 8716288 | tf_op jit(solution)/shard_map/project/pallas_call | solution.py:229
  481.3 16.5 %project.13 = (bf16[2,128,4608]{2,1,0:T(8,128)(2,1)}, bf16[4,4608,128]{2,1,0:T(8,128)(2,1)}, bf16[4,128,4608]{2,1,0:T(8,128)(2,1)}) custom-call(s32[5]{0:T(128)S(1)} %concatenate.72.spot_ref, bf16[512,2432]{1,0:T(8,128)(2,1)} %collective-permute-done.12.refs_0_, ...), custom_call_target="tpu_custom_call", output_to_operand_aliasing={{0}: (11, {}), {1}: (12, {}), {2}: (13, {})} | custom-call | flops 7650410496 | bytes 13697024 | tf_op jit(solution)/shard_map/project/pallas_call | solution.py:229
  497.8 11.8 %project.14 = (bf16[2,128,4608]{2,1,0:T(8,128)(2,1)}, bf16[4,4608,128]{2,1,0:T(8,128)(2,1)}, bf16[4,128,4608]{2,1,0:T(8,128)(2,1)}) custom-call(s32[5]{0:T(128)S(1)} %concatenate.71.spot_ref, bf16[512,2432]{1,0:T(8,128)(2,1)} %collective-permute-done.18.refs_0_, ...), custom_call_target="tpu_custom_call", output_to_operand_aliasing={{0}: (11, {}), {1}: (12, {}), {2}: (13, {})} | custom-call | flops 7650410496 | bytes 13697024 | tf_op jit(solution)/shard_map/project/pallas_call | solution.py:229
  520.0 9.3 %attend.11 = bf16[256,256]{1,0:T(8,128)(2,1)S(1)} custom-call(s32[1]{0:T(128)} %get-tuple-element.116.len_ref, bf16[2,128,256]{2,1,0:T(8,128)(2,1)S(1)} %copy-done.19, bf16[4,4608,128]{2,1,0:T(8,128)(2,1)S(1)} %copy-done.22, bf16[4,128,4608]{2,1,0:T(8,128)(2,1)} %get-tuple-element.79.v_ref, bf16[4,256,128]{2,1,0:T(8,128)(2,1)S(1)} %copy-done.14, ...), custom_call_target="tpu_custom_call" | custom-call | flops 4294967296 | bytes 8388608 | tf_op jit(solution)/shard_map/attend/pallas_call | solution.py:66
  531.6 6.1 all-to-all-start.5
  539.4 21.8 %attend.9 = bf16[4096,128]{1,0:T(8,128)(2,1)S(1)} custom-call(s32[1]{0:T(128)} %get-tuple-element.116.len_ref, bf16[2,128,4608]{2,1,0:T(8,128)(2,1)S(1)} %copy-done.24, bf16[4,4608,128]{2,1,0:T(8,128)(2,1)} %get-tuple-element.78.k_ref, bf16[4,128,4608]{2,1,0:T(8,128)(2,1)} %get-tuple-element.79.v_ref, bf16[4,256,128]{2,1,0:T(8,128)(2,1)S(1)} %copy-done.15, ...), custom_call_target="tpu_custom_call" | custom-call | flops 34359738368 | bytes 4194304 | tf_op jit(solution)/shard_map/attend/pallas_call | solution.py:66
  570.7 21.8 %attend.8 = bf16[4096,128]{1,0:T(8,128)(2,1)S(1)} custom-call(s32[1]{0:T(128)} %get-tuple-element.116.len_ref, bf16[2,128,4608]{2,1,0:T(8,128)(2,1)S(1)} %copy-done.25, bf16[4,4608,128]{2,1,0:T(8,128)(2,1)} %get-tuple-element.78.k_ref, bf16[4,128,4608]{2,1,0:T(8,128)(2,1)} %get-tuple-element.79.v_ref, bf16[4,256,128]{2,1,0:T(8,128)(2,1)S(1)} %copy-done.16, ...), custom_call_target="tpu_custom_call" | custom-call | flops 34359738368 | bytes 4194304 | tf_op jit(solution)/shard_map/attend/pallas_call | solution.py:66
  602.6 23.0 %all-to-all-done.2.refs_0_ = bf16[8,512,128]{2,1,0:T(8,128)(2,1)} async-done(((bf16[8,512,128]{2,1,0:T(8,128)(2,1)}), bf16[8,512,128]{2,1,0:T(8,128)(2,1)}, u32[]{:S(2)}, u32[]{:S(2)}) %all-to-all-start.2) | async-done | bytes 1048608 | tf_op jit(solution)/shard_map/all_to_all | solution.py:530
  (237 shorter events, 181.3 us)
Async XLA Ops:
  8.5 173.9 %collective-permute-start.11 = (bf16[512,2432]{1,0:T(8,128)(2,1)}, bf16[512,2432]{1,0:T(8,128)(2,1)}, u32[]{:S(2)}, u32[]{:S(2)}) collective-permute-start(bf16[512,2432]{1,0:T(8,128)(2,1)} %get-tuple-element.88.refs_0_), channel_id=1, source_target_pairs={{0,1},{1,0},{2,3},{3,2},{4,5},{5,4},{6,7},{7,6},{8,9},{9,8},{10,11... | collective-permute-start | bytes 7471112 | tf_op jit(solution)/shard_map/ppermute | solution.py:373
  8.9 65.5 %collective-permute-start = (bf16[512,2432]{1,0:T(8,128)(2,1)}, bf16[512,2432]{1,0:T(8,128)(2,1)}, u32[]{:S(2)}, u32[]{:S(2)}) collective-permute-start(bf16[512,2432]{1,0:T(8,128)(2,1)} %get-tuple-element.88.refs_0_), channel_id=1, source_target_pairs={{0,2},{1,3},{2,4},{3,5},{4,6},{5,7},{8,10},{9,11},{10,12},{11,13},... | collective-permute-start | bytes 7471112 | tf_op jit(solution)/shard_map/ppermute | solution.py:380
  14.8 59.7 %collective-permute-start.1 = (bf16[512,2432]{1,0:T(8,128)(2,1)}, bf16[512,2432]{1,0:T(8,128)(2,1)}, u32[]{:S(2)}, u32[]{:S(2)}) collective-permute-start(bf16[512,2432]{1,0:T(8,128)(2,1)} %get-tuple-element.88.refs_0_), channel_id=1, source_target_pairs={{2,0},{3,1},{4,2},{5,3},{6,4},{7,5},{10,8},{11,9},{12,10},{13,11},... | collective-permute-start | bytes 7471112 | tf_op jit(solution)/shard_map/ppermute | solution.py:381
  27.6 118.6 %collective-permute-start.8 = (bf16[2432,192]{0,1:T(8,128)(2,1)}, bf16[2432,192]{0,1:T(8,128)(2,1)}, u32[]{:S(2)}, u32[]{:S(2)}) collective-permute-start(bf16[2432,192]{0,1:T(8,128)(2,1)} %param.20), channel_id=1, source_target_pairs={{0,8},{8,0},{16,24},{24,16},{1,9},{9,1},{17,25},{25,17},{2,10},{10... | collective-permute-start | bytes 2801672 | tf_op jit(solution)/shard_map/ppermute | solution.py:294
  78.6 57.6 %collective-permute-start.3 = (bf16[512,2432]{1,0:T(8,128)(2,1)}, bf16[512,2432]{1,0:T(8,128)(2,1)}, u32[]{:S(2)}, u32[]{:S(2)}) collective-permute-start(bf16[512,2432]{1,0:T(8,128)(2,1)} %collective-permute-done.1.refs_2_), channel_id=1, source_target_pairs={{2,0},{3,1},{4,2},{5,3},{6,4},{7,5},{10,8},{11,9},{12,10},{13,11},... | collective-permute-start | bytes 7471112 | tf_op jit(solution)/shard_map/ppermute | solution.py:381
  87.3 95.8 %collective-permute-start.6 = (bf16[512,2432]{1,0:T(8,128)(2,1)}, bf16[512,2432]{1,0:T(8,128)(2,1)}, u32[]{:S(2)}, u32[]{:S(2)}) collective-permute-start(bf16[512,2432]{1,0:T(8,128)(2,1)} %collective-permute-done.refs_0_), channel_id=1, source_target_pairs={{0,1},{1,0},{2,3},{3,2},{4,5},{5,4},{6,7},{7,6},{8,9},{9,8},{10,11... | collective-permute-start | bytes 7471112 | tf_op jit(solution)/shard_map/ppermute | solution.py:373
  146.2 88.0 %collective-permute-start.7 = (bf16[512,2432]{1,0:T(8,128)(2,1)}, bf16[512,2432]{1,0:T(8,128)(2,1)}, u32[]{:S(2)}, u32[]{:S(2)}) collective-permute-start(bf16[512,2432]{1,0:T(8,128)(2,1)} %collective-permute-done.1.refs_2_), channel_id=1, source_target_pairs={{0,1},{1,0},{2,3},{3,2},{4,5},{5,4},{6,7},{7,6},{8,9},{9,8},{10,11... | collective-permute-start | bytes 7471112 | tf_op jit(solution)/shard_map/ppermute | solution.py:373
  182.4 82.4 %collective-permute-start.16 = (bf16[512,2432]{1,0:T(8,128)(2,1)}, bf16[512,2432]{1,0:T(8,128)(2,1)}, u32[]{:S(2)}, u32[]{:S(2)}) collective-permute-start(bf16[512,2432]{1,0:T(8,128)(2,1)} %collective-permute-done.2.refs_0_), channel_id=1, source_target_pairs={{0,1},{1,0},{2,3},{3,2},{4,5},{5,4},{6,7},{7,6},{8,9},{9,8},{10,11... | collective-permute-start | bytes 7471112 | tf_op jit(solution)/shard_map/ppermute | solution.py:373
  183.1 94.8 %collective-permute-start.17 = (bf16[512,2432]{1,0:T(8,128)(2,1)}, bf16[512,2432]{1,0:T(8,128)(2,1)}, u32[]{:S(2)}, u32[]{:S(2)}) collective-permute-start(bf16[512,2432]{1,0:T(8,128)(2,1)} %collective-permute-done.3.refs_2_), channel_id=1, source_target_pairs={{0,1},{1,0},{2,3},{3,2},{4,5},{5,4},{6,7},{7,6},{8,9},{9,8},{10,11... | collective-permute-start | bytes 7471112 | tf_op jit(solution)/shard_map/ppermute | solution.py:373
  228.6 67.4 %collective-permute-start.14 = (bf16[512,2432]{1,0:T(8,128)(2,1)}, bf16[512,2432]{1,0:T(8,128)(2,1)}, u32[]{:S(2)}, u32[]{:S(2)}) collective-permute-start(bf16[512,2432]{1,0:T(8,128)(2,1)} %collective-permute-done.4.refs_0_), channel_id=1, source_target_pairs={{0,1},{1,0},{2,3},{3,2},{4,5},{5,4},{6,7},{7,6},{8,9},{9,8},{10,11... | collective-permute-start | bytes 7471112 | tf_op jit(solution)/shard_map/ppermute | solution.py:373
  234.1 61.8 %collective-permute-start.15 = (bf16[512,2432]{1,0:T(8,128)(2,1)}, bf16[512,2432]{1,0:T(8,128)(2,1)}, u32[]{:S(2)}, u32[]{:S(2)}) collective-permute-start(bf16[512,2432]{1,0:T(8,128)(2,1)} %collective-permute-done.5.refs_2_), channel_id=1, source_target_pairs={{0,1},{1,0},{2,3},{3,2},{4,5},{5,4},{6,7},{7,6},{8,9},{9,8},{10,11... | collective-permute-start | bytes 7471112 | tf_op jit(solution)/shard_map/ppermute | solution.py:373
  250.6 67.1 %collective-permute-start.12 = (bf16[512,2432]{1,0:T(8,128)(2,1)}, bf16[512,2432]{1,0:T(8,128)(2,1)}, u32[]{:S(2)}, u32[]{:S(2)}) collective-permute-start(bf16[512,2432]{1,0:T(8,128)(2,1)} %get-tuple-element.66.refs_0_), channel_id=1, source_target_pairs={{0,2},{1,3},{2,4},{3,5},{4,6},{5,7},{8,10},{9,11},{10,12},{11,13},... | collective-permute-start | bytes 7471112 | tf_op jit(solution)/shard_map/ppermute | solution.py:380
  264.9 58.4 %collective-permute-start.13 = (bf16[512,2432]{1,0:T(8,128)(2,1)}, bf16[512,2432]{1,0:T(8,128)(2,1)}, u32[]{:S(2)}, u32[]{:S(2)}) collective-permute-start(bf16[512,2432]{1,0:T(8,128)(2,1)} %get-tuple-element.66.refs_0_), channel_id=1, source_target_pairs={{2,0},{3,1},{4,2},{5,3},{6,4},{7,5},{10,8},{11,9},{12,10},{13,11},... | collective-permute-start | bytes 7471112 | tf_op jit(solution)/shard_map/ppermute | solution.py:381
  277.9 109.9 %collective-permute-start.28 = (bf16[512,2432]{1,0:T(8,128)(2,1)}, bf16[512,2432]{1,0:T(8,128)(2,1)S(1)}, u32[]{:S(2)}, u32[]{:S(2)}) collective-permute-start(bf16[512,2432]{1,0:T(8,128)(2,1)} %get-tuple-element.66.refs_0_), channel_id=1, source_target_pairs={{0,1},{1,0},{2,3},{3,2},{4,5},{5,4},{6,7},{7,6},{8,9},{9,8},{10,11... | collective-permute-start | bytes 7471112 | tf_op jit(solution)/shard_map/ppermute | solution.py:373
  326.2 57.4 %collective-permute-start.19 = (bf16[512,2432]{1,0:T(8,128)(2,1)}, bf16[512,2432]{1,0:T(8,128)(2,1)}, u32[]{:S(2)}, u32[]{:S(2)}) collective-permute-start(bf16[512,2432]{1,0:T(8,128)(2,1)} %collective-permute-done.13.refs_2_), channel_id=1, source_target_pairs={{2,0},{3,1},{4,2},{5,3},{6,4},{7,5},{10,8},{11,9},{12,10},{13,11},... | collective-permute-start | bytes 7471112 | tf_op jit(solution)/shard_map/ppermute | solution.py:381
  327.7 60.2 %collective-permute-start.26 = (bf16[512,2432]{1,0:T(8,128)(2,1)}, bf16[512,2432]{1,0:T(8,128)(2,1)S(1)}, u32[]{:S(2)}, u32[]{:S(2)}) collective-permute-start(bf16[512,2432]{1,0:T(8,128)(2,1)} %collective-permute-done.12.refs_0_), channel_id=1, source_target_pairs={{0,1},{1,0},{2,3},{3,2},{4,5},{5,4},{6,7},{7,6},{8,9},{9,8},{10,11... | collective-permute-start | bytes 7471112 | tf_op jit(solution)/shard_map/ppermute | solution.py:373
  366.8 114.5 %collective-permute-start.27 = (bf16[512,2432]{1,0:T(8,128)(2,1)}, bf16[512,2432]{1,0:T(8,128)(2,1)}, u32[]{:S(2)}, u32[]{:S(2)}) collective-permute-start(bf16[512,2432]{1,0:T(8,128)(2,1)} %collective-permute-done.13.refs_2_), channel_id=1, source_target_pairs={{0,1},{1,0},{2,3},{3,2},{4,5},{5,4},{6,7},{7,6},{8,9},{9,8},{10,11... | collective-permute-start | bytes 7471112 | tf_op jit(solution)/shard_map/ppermute | solution.py:373
  383.6 56.3 %collective-permute-start.20 = (bf16[512,2432]{1,0:T(8,128)(2,1)}, bf16[512,2432]{1,0:T(8,128)(2,1)}, u32[]{:S(2)}, u32[]{:S(2)}) collective-permute-start(bf16[512,2432]{1,0:T(8,128)(2,1)} %collective-permute-done.18.refs_0_), channel_id=1, source_target_pairs={{0,2},{1,3},{2,4},{3,5},{4,6},{5,7},{8,10},{9,11},{10,12},{11,13},... | collective-permute-start | bytes 7471112 | tf_op jit(solution)/shard_map/ppermute | solution.py:380
  386.5 62.0 %collective-permute-start.22 = (bf16[512,2432]{1,0:T(8,128)(2,1)}, bf16[512,2432]{1,0:T(8,128)(2,1)}, u32[]{:S(2)}, u32[]{:S(2)}) collective-permute-start(bf16[512,2432]{1,0:T(8,128)(2,1)} %collective-permute-done.19.refs_2_), channel_id=1, source_target_pairs={{2,0},{3,1},{4,2},{5,3},{6,4},{7,5},{10,8},{11,9},{12,10},{13,11},... | collective-permute-start | bytes 7471112 | tf_op jit(solution)/shard_map/ppermute | solution.py:381
  387.8 110.0 %collective-permute-start.24 = (bf16[512,2432]{1,0:T(8,128)(2,1)}, bf16[512,2432]{1,0:T(8,128)(2,1)}, u32[]{:S(2)}, u32[]{:S(2)}) collective-permute-start(bf16[512,2432]{1,0:T(8,128)(2,1)} %collective-permute-done.18.refs_0_), channel_id=1, source_target_pairs={{0,1},{1,0},{2,3},{3,2},{4,5},{5,4},{6,7},{7,6},{8,9},{9,8},{10,11... | collective-permute-start | bytes 7471112 | tf_op jit(solution)/shard_map/ppermute | solution.py:373
  387.9 109.9 %collective-permute-start.25 = (bf16[512,2432]{1,0:T(8,128)(2,1)}, bf16[512,2432]{1,0:T(8,128)(2,1)}, u32[]{:S(2)}, u32[]{:S(2)}) collective-permute-start(bf16[512,2432]{1,0:T(8,128)(2,1)} %collective-permute-done.19.refs_2_), channel_id=1, source_target_pairs={{0,1},{1,0},{2,3},{3,2},{4,5},{5,4},{6,7},{7,6},{8,9},{9,8},{10,11... | collective-permute-start | bytes 7471112 | tf_op jit(solution)/shard_map/ppermute | solution.py:373
  427.5 104.1 %all-to-all-start.4 = ((bf16[8,512,256]{2,1,0:T(8,128)(2,1)}), bf16[8,512,256]{2,1,0:T(8,128)(2,1)S(1)}, u32[]{:S(2)}, u32[]{:S(2)}) async-start(bf16[8,512,256]{2,1,0:T(8,128)(2,1)} %bitcast.119), calls=%async_computation.4 | async-start | bytes 4194304 | tf_op jit(solution)/shard_map/all_to_all | solution.py:530
  439.9 69.7 %collective-permute-start.21 = (bf16[512,2432]{1,0:T(8,128)(2,1)}, bf16[512,2432]{1,0:T(8,128)(2,1)S(1)}, u32[]{:S(2)}, u32[]{:S(2)}) collective-permute-start(bf16[512,2432]{1,0:T(8,128)(2,1)} %collective-permute-done.20.refs_0_), channel_id=1, source_target_pairs={{0,1},{1,0},{2,3},{3,2},{4,5},{5,4},{6,7},{7,6},{8,9},{9,8},{10,11... | collective-permute-start | bytes 7471112 | tf_op jit(solution)/shard_map/ppermute | solution.py:373
  448.5 61.1 %collective-permute-start.23 = (bf16[512,2432]{1,0:T(8,128)(2,1)}, bf16[512,2432]{1,0:T(8,128)(2,1)S(1)}, u32[]{:S(2)}, u32[]{:S(2)}) collective-permute-start(bf16[512,2432]{1,0:T(8,128)(2,1)} %collective-permute-done.22.refs_2_), channel_id=1, source_target_pairs={{0,1},{1,0},{2,3},{3,2},{4,5},{5,4},{6,7},{7,6},{8,9},{9,8},{10,11... | collective-permute-start | bytes 7471112 | tf_op jit(solution)/shard_map/ppermute | solution.py:373
  (54 other events, 1199.8 us)
